TPU v7x, 32 devices: a whole 2x2x4 slice. The times are simulated.
32 devices in a mesh: pts: 4 (over x, core), snap: 8 (over z, y).
Axes of the slice: x: 2, y: 2, z: 4, core: 2. Of those that a mesh axis runs over, the one named last changes fastest.
Arguments:
- snapshots: bfloat16 [1024, 3, 16384], P('snap', None, 'pts')
- block_starts: int32 [31], replicated, may hold values from 0 to 960, as said below
- point_slab: int32 [16384], P(('pts', 'snap')), may hold values from 0 to 15
- slab_weight: float32 [16], replicated, may hold values from 1 to 10
Outputs:
- mode_field: bfloat16 [2, 33, 31, 3, 16384], P(None, None, None, None, ('pts', 'snap'))
- r_factor: float32 [2, 33, 31, 31], replicated
Inputs may be any that keep to these rules, and one draw needn't show every extreme that they name: `block_starts`: strictly increasing; the first is 0 and the last is 960; neighbours lie more than 16 apart.
All inputs are finite; a program needn't handle non-finite values.
Results may differ from a plain program's by a relative error of at most 0.0017.
The roundings to bfloat16 on the way count: a program that leaves them out, or rounds other values in their place, can miss the bound.
Values may be sent and summed in bfloat16 or wider, within the bound.
A program may use at most 128 MiB of HBM per device.

v0:
```python
import math

import jax
import jax.numpy as jnp
from jax import lax
from jax.sharding import PartitionSpec as P

NT = 1024
WIN = 64


def make_tables(length, freq_count):
    steps_time = jnp.arange(length, dtype=jnp.int32)
    freq_index = jnp.arange(freq_count, dtype=jnp.int32)
    phase_index = freq_index[:, None] * steps_time[None, :] % length
    angle_value = 2.0 * math.pi / length * phase_index.astype(jnp.float32)
    window = 0.5 - 0.5 * jnp.cos(2.0 * math.pi / length * steps_time.astype(jnp.float32))
    dft_table = jnp.stack(
        [window[None, :] * jnp.cos(angle_value), -window[None, :] * jnp.sin(angle_value)]
    ).astype(jnp.bfloat16)
    row_sums = jnp.sum(dft_table.astype(jnp.float32), axis=2)
    return (dft_table, row_sums)


def spectra(series, starts, dft_table, row_sums):
    blocks = jax.vmap(lambda offset: lax.dynamic_slice_in_dim(series, offset, WIN, 0))(starts)
    raw_spec = jnp.einsum("kfw,bwcp->kfbcp", dft_table, blocks, preferred_element_type=jnp.float32)
    time_mean = jnp.sum(series.astype(jnp.float32), axis=0) / NT
    return raw_spec - row_sums[:, :, None, None, None] * time_mean[None, None, None]


def gram(amplitude):
    highest = lax.Precision.HIGHEST
    amp_real, amp_imag = (amplitude[0], amplitude[1])
    part_real = jnp.einsum("fbn,fdn->bdf", amp_real, amp_real, precision=highest) + jnp.einsum(
        "fbn,fdn->bdf", amp_imag, amp_imag, precision=highest
    )
    part_imag = jnp.einsum("fbn,fdn->bdf", amp_real, amp_imag, precision=highest) - jnp.einsum(
        "fbn,fdn->bdf", amp_imag, amp_real, precision=highest
    )
    return (part_real, part_imag)


def complex_cholesky(gram_real, gram_imag):
    size_n = gram_real.shape[0]
    positions = jnp.arange(size_n, dtype=jnp.int32)
    rows_real = []
    rows_imag = []
    for column in range(size_n):
        rest_real = gram_real[column]
        rest_imag = gram_imag[column]
        if column > 0:
            done_real = jnp.stack(rows_real)
            done_imag = jnp.stack(rows_imag)
            above_real = done_real[:, column]
            above_imag = done_imag[:, column]
            rest_real = rest_real - jnp.sum(
                above_real[:, None] * done_real + above_imag[:, None] * done_imag, axis=0
            )
            rest_imag = rest_imag - jnp.sum(
                above_real[:, None] * done_imag - above_imag[:, None] * done_real, axis=0
            )
        pivot_value = jnp.sqrt(rest_real[column])
        keep_real = (positions >= column)[:, None]
        keep_imag = (positions > column)[:, None]
        rows_real.append(jnp.where(keep_real, rest_real / pivot_value, jnp.zeros_like(rest_real)))
        rows_imag.append(jnp.where(keep_imag, rest_imag / pivot_value, jnp.zeros_like(rest_imag)))
    return (jnp.stack(rows_real), jnp.stack(rows_imag))


def upper_inverse(upper_real, upper_imag):
    size_n = upper_real.shape[0]
    identity = jnp.eye(size_n, dtype=upper_real.dtype)
    rows_real = []
    rows_imag = []
    for row_index in reversed(range(size_n)):
        rest_real = jnp.broadcast_to(identity[row_index][:, None], upper_real.shape[1:])
        rest_imag = jnp.zeros_like(rest_real)
        if row_index < size_n - 1:
            done_real = jnp.stack(rows_real[::-1])
            done_imag = jnp.stack(rows_imag[::-1])
            coef_real = upper_real[row_index, row_index + 1 :]
            coef_imag = upper_imag[row_index, row_index + 1 :]
            rest_real = rest_real - jnp.sum(
                coef_real[:, None] * done_real - coef_imag[:, None] * done_imag, axis=0
            )
            rest_imag = rest_imag - jnp.sum(
                coef_real[:, None] * done_imag + coef_imag[:, None] * done_real, axis=0
            )
        pivot_value = upper_real[row_index, row_index]
        rows_real.append(rest_real / pivot_value)
        rows_imag.append(rest_imag / pivot_value)
    return (jnp.stack(rows_real[::-1]), jnp.stack(rows_imag[::-1]))


def project(amplitude, inv_real, inv_imag):
    highest = lax.Precision.HIGHEST
    amp_real, amp_imag = (amplitude[0], amplitude[1])
    mode_real = jnp.einsum("fbn,bmf->fmn", amp_real, inv_real, precision=highest) - jnp.einsum(
        "fbn,bmf->fmn", amp_imag, inv_imag, precision=highest
    )
    mode_imag = jnp.einsum("fbn,bmf->fmn", amp_real, inv_imag, precision=highest) + jnp.einsum(
        "fbn,bmf->fmn", amp_imag, inv_real, precision=highest
    )
    return jnp.stack([mode_real, mode_imag])


def on_device(snapshots, block_starts, point_slab, slab_weight):
    dft_table, row_sums = make_tables(WIN, WIN // 2 + 1)
    series = lax.all_to_all(snapshots, "snap", split_axis=2, concat_axis=0, tiled=True)
    spectrum = spectra(series, block_starts, dft_table, row_sums)
    freq_count = spectrum.shape[1]
    block_count = spectrum.shape[2]
    points = spectrum.shape[4]
    all_points = points * lax.axis_size("pts") * lax.axis_size("snap")
    slab_ids = jnp.arange(slab_weight.shape[0], dtype=jnp.int32)
    one_hot = (point_slab[:, None] == slab_ids[None, :]).astype(jnp.float32)
    weights = jnp.dot(one_hot, slab_weight, precision=lax.Precision.HIGHEST)
    root_weight = jnp.sqrt(weights / (0.375 * WIN))
    amplitude = (spectrum * root_weight).reshape(2, freq_count, block_count, 3 * points)
    part_real, part_imag = gram(amplitude)
    norm_scale = 1.0 / (3.0 * all_points)
    sum_real, sum_imag = lax.psum((part_real, part_imag), ("pts", "snap"))
    upper_real, upper_imag = complex_cholesky(sum_real * norm_scale, sum_imag * norm_scale)
    inv_real, inv_imag = upper_inverse(upper_real, upper_imag)
    mode_field = (
        project(amplitude, inv_real, inv_imag)
        .reshape(2, freq_count, block_count, 3, points)
        .astype(jnp.bfloat16)
    )
    r_factor = jnp.transpose(jnp.stack([upper_real, upper_imag]), (0, 3, 1, 2))
    return (mode_field, r_factor)


def solution(mesh):
    in_specs = (P("snap", None, "pts"), P(), P(("pts", "snap")), P())
    out_specs = (P(None, None, None, None, ("pts", "snap")), P())
    return jax.shard_map(
        on_device, mesh=mesh, in_specs=in_specs, out_specs=out_specs, check_vma=False
    )
```

profile of v0, /device:TPU:0, one launch (start us, length us, event | category | flops | bytes accessed | tf_op | source)
XLA Modules:
  0.0 538.7 jit_solution(13865715514049991911)
XLA Ops:
  7.2 7.2 %copy.17234 = bf16[128,3,4096]{0,1,2:T(4,128)(2,1)} copy(bf16[128,3,4096]{2,0,1:T(8,128)(2,1)} %param.4) | data formatting | bytes 6291456 | tf_op args[0]
  14.4 7.3 %all-to-all-start = ((bf16[128,3,4096]{0,1,2:T(4,128)(2,1)}), bf16[128,3,4096]{0,1,2:T(4,128)(2,1)}, u32[]{:S(2)}, u32[]{:S(2)}) async-start(bf16[128,3,4096]{0,1,2:T(4,128)(2,1)} %copy.17234), calls=%async_computation | async-start | bytes 8388608 | tf_op jit(solution)/shard_map/all_to_all | solution.py:110
  22.8 92.2 %all-to-all-done = bf16[128,3,4096]{0,1,2:T(4,128)(2,1)} async-done(((bf16[128,3,4096]{0,1,2:T(4,128)(2,1)}), bf16[128,3,4096]{0,1,2:T(4,128)(2,1)}, u32[]{:S(2)}, u32[]{:S(2)}) %all-to-all-start) | async-done | bytes 3145760 | tf_op jit(solution)/shard_map/all_to_all | solution.py:110
  120.1 4.7 copy.17236
  124.9 11.6 %gather_fusion = bf16[31,64,3,512]{3,2,1,0:T(4,128)(2,1)} fusion(bf16[1024,3,512]{2,1,0:T(4,128)(2,1)} %bitcast.631, s32[31]{0:T(128)S(1)} %fusion.108), kind=kCustom, calls=%fused_computation | custom fusion | bytes 12190068 | tf_op jit(solution)/shard_map/vmap()/gather | solution.py:26
  136.5 11.4 %subtract_multiply_fusion = f32[2,33,31,3,512]{4,1,3,2,0:T(8,128)} fusion(f32[512]{0:T(512)S(1)} %multiply_sqrt_fusion, f32[2,33,3,512]{3,1,2,0:T(8,128)S(1)} %broadcast_multiply_fusion.2, bf16[31,64,3,512]{3,2,1,0:T(4,128)(2,1)} %gather_fusion, bf16[1,33,64]{2,1,0:T(8,128)(2,1)S(1)} %get-tuple-element.379, bf16[1,33,64]{2,1,0:T(8,128)(2,1)S(1)} %get-tuple-element.380), kind=kOutput, calls=%fused_computation.1 | convolution fusion | flops 408562176 | bytes 19081472 | tf_op jit(solution)/shard_map/kfw,bwcp->kfbcp/dot_general | solution.py:27
  147.9 12.5 %fusion.116 = (f32[1,33,31,3,512]{4,1,3,2,0:T(8,128)}, f32[1,33,31,3,512]{4,1,3,2,0:T(8,128)}) fusion(f32[2,33,31,3,512]{4,1,3,2,0:T(8,128)} %subtract_multiply_fusion), kind=kLoop, calls=%fused_computation.928 | loop fusion | bytes 25141248 | tf_op jit(solution)/shard_map/slice | solution.py:34
  160.4 10.7 %copy.17238 = f32[1,33,31,3,512]{4,3,2,1,0:T(4,128)} copy(f32[1,33,31,3,512]{4,1,3,2,0:T(8,128)} %get-tuple-element.190) | data formatting | bytes 12570624 | tf_op jit(solution)/shard_map/slice | solution.py:34
  171.1 11.8 %squeeze.62 = f32[33,31,1536]{2,1,0:T(8,128)} reshape(f32[1,33,31,3,512]{4,3,2,1,0:T(4,128)} %copy.17238) | data formatting | bytes 12570624 | tf_op jit(solution)/shard_map/squeeze | solution.py:34
  182.9 10.7 %copy.17239 = f32[1,33,31,3,512]{4,3,2,1,0:T(4,128)} copy(f32[1,33,31,3,512]{4,1,3,2,0:T(8,128)} %get-tuple-element.191) | data formatting | bytes 12570624 | tf_op jit(solution)/shard_map/slice | solution.py:34
  193.6 11.4 %squeeze.63 = f32[33,31,1536]{2,1,0:T(8,128)} reshape(f32[1,33,31,3,512]{4,3,2,1,0:T(4,128)} %copy.17239) | data formatting | bytes 12570624 | tf_op jit(solution)/shard_map/squeeze | solution.py:34
  205.0 9.4 %fusion.123 = f32[33,31,31]{2,1,0:T(8,128)S(1)} fusion(f32[33,31,1536]{2,1,0:T(8,128)} %squeeze.62, f32[33,31,1536]{2,1,0:T(8,128)} %squeeze.63), kind=kOutput, calls=%fused_computation.935 | convolution fusion | flops 584534016 | bytes 12697476 | tf_op jit(solution)/shard_map/fbn,fdn->bdf/dot_general | solution.py:38
  214.4 6.0 %fusion.122 = f32[33,31,31]{2,1,0:T(8,128)S(1)} fusion(f32[33,31,1536]{2,1,0:T(8,128)S(1)} %copy-done.3, f32[33,31,1536]{2,1,0:T(8,128)S(1)} %copy-done.2), kind=kOutput, calls=%fused_computation.934 | convolution fusion | flops 584534016 | bytes 12697476 | tf_op jit(solution)/shard_map/fbn,fdn->bdf/dot_general | solution.py:38
  220.4 6.4 %fusion.120 = f32[33,31,31]{2,1,0:T(8,128)S(1)} fusion(f32[33,31,1536]{2,1,0:T(8,128)S(1)} %copy-done.2), kind=kOutput, calls=%fused_computation.932 | convolution fusion | flops 584534016 | bytes 6412164 | tf_op jit(solution)/shard_map/fbn,fdn->bdf/dot_general | solution.py:35
  226.8 6.1 %fusion.121 = f32[33,31,31]{2,1,0:T(8,128)S(1)} fusion(f32[33,31,1536]{2,1,0:T(8,128)S(1)} %copy-done.3), kind=kOutput, calls=%fused_computation.933 | convolution fusion | flops 584534016 | bytes 6412164 | tf_op jit(solution)/shard_map/fbn,fdn->bdf/dot_general | solution.py:35
  236.6 128.7 %all-reduce.4.cloned.1.call-done = (f32[31,31,33]{2,0,1:T(8,128)}, f32[31,31,33]{2,0,1:T(8,128)}) async-done(((f32[31,31,33]{2,0,1:T(8,128)}, f32[31,31,33]{2,0,1:T(8,128)}), (f32[31,31,33]{2,0,1:T(8,128)}, f32[31,31,33]{2,0,1:T(8,128)})) %all-reduce.4.cloned.1.call-update) | async-done | bytes 253720 | tf_op jit(solution)/shard_map/psum | solution.py:123
  462.8 9.6 %fusion.124 = f32[33,31,1536]{2,1,0:T(8,128)} fusion(f32[31,31,33]{0,1,2:T(8,128)S(1)} %copy.17831, f32[33,31,1536]{2,1,0:T(8,128)} %squeeze.62), kind=kOutput, calls=%fused_computation.936 | convolution fusion | flops 584534016 | bytes 12697476 | tf_op jit(solution)/shard_map/fbn,bmf->fmn/dot_general | solution.py:99
  473.8 9.6 %fusion.125 = f32[33,31,1536]{2,1,0:T(8,128)} fusion(f32[31,31,33]{0,1,2:T(8,128)S(1)} %copy.17835, f32[33,31,1536]{2,1,0:T(8,128)} %squeeze.62), kind=kOutput, calls=%fused_computation.937 | convolution fusion | flops 584534016 | bytes 12697476 | tf_op jit(solution)/shard_map/fbn,bmf->fmn/dot_general | solution.py:102
  483.4 9.5 %subtract_convert_fusion = bf16[33,31,1536]{2,1,0:T(8,128)(2,1)} fusion(f32[33,31,1536]{2,1,0:T(8,128)S(1)} %bitcast.634, f32[31,31,33]{0,1,2:T(8,128)S(1)} %copy.17835, f32[33,31,1536]{2,1,0:T(8,128)} %squeeze.63), kind=kOutput, calls=%fused_computation.4 | convolution fusion | flops 587676672 | bytes 15840132 | tf_op jit(solution)/shard_map/fbn,bmf->fmn/dot_general | solution.py:99
  492.9 8.7 %stack.380 = bf16[1,33,31,3,512]{4,3,2,1,0:T(4,128)(2,1)} reshape(bf16[33,31,1536]{2,1,0:T(8,128)(2,1)} %subtract_convert_fusion) | data formatting | bytes 6285312 | tf_op jit(solution)/shard_map/stack | solution.py:105
  501.6 8.9 %add_convert_fusion = bf16[33,31,1536]{2,1,0:T(8,128)(2,1)S(1)} fusion(f32[33,31,1536]{2,1,0:T(8,128)} %fusion.125, f32[31,31,33]{0,1,2:T(8,128)} %copy-done.5, f32[33,31,1536]{2,1,0:T(8,128)} %squeeze.63), kind=kOutput, calls=%fused_computation.3 | convolution fusion | flops 587676672 | bytes 15840132 | tf_op jit(solution)/shard_map/fbn,bmf->fmn/dot_general | solution.py:102
  510.6 5.8 %stack.381 = bf16[1,33,31,3,512]{4,3,2,1,0:T(4,128)(2,1)} reshape(bf16[33,31,1536]{2,1,0:T(8,128)(2,1)S(1)} %add_convert_fusion) | data formatting | bytes 6285312 | tf_op jit(solution)/shard_map/stack | solution.py:105
  516.4 7.6 %pad_maximum_fusion = bf16[2,33,31,3,512]{4,3,2,1,0:T(4,128)(2,1)S(1)} fusion(bf16[1,33,31,3,512]{4,3,2,1,0:T(4,128)(2,1)} %stack.381, bf16[1,33,31,3,512]{4,3,2,1,0:T(4,128)(2,1)} %stack.380), kind=kLoop, calls=%fused_computation.2 | loop fusion | flops 3142656 | bytes 12570624 | tf_op jit(solution)/shard_map/stack | solution.py:105
  524.0 7.6 %copy.17843 = bf16[2,33,31,3,512]{4,0,3,2,1:T(2,128)(2,1)} copy(bf16[2,33,31,3,512]{4,3,2,1,0:T(4,128)(2,1)S(1)} %pad_maximum_fusion) | data formatting | bytes 12570624
  (976 shorter events, 104.1 us)
Async XLA Ops:
  7.2 15.2 %copy-start = (f32[16]{0:T(128)S(1)}, f32[16]{0:T(128)}, u32[]{:S(2)}) copy-start(f32[16]{0:T(128)} %param.7) | copy-start | bytes 196
  7.2 15.2 %copy-start.7 = (s32[31]{0:T(128)S(1)}, s32[31]{0:T(128)}, u32[]{:S(2)}) copy-start(s32[31]{0:T(128)} %param.5) | copy-start | bytes 376
  7.2 15.2 %copy-start.6 = (s32[512]{0:T(512)S(1)}, s32[512]{0:T(512)}, u32[]{:S(2)}) copy-start(s32[512]{0:T(512)} %param.6) | copy-start | bytes 6148
  14.4 100.6 %all-to-all-start = ((bf16[128,3,4096]{0,1,2:T(4,128)(2,1)}), bf16[128,3,4096]{0,1,2:T(4,128)(2,1)}, u32[]{:S(2)}, u32[]{:S(2)}) async-start(bf16[128,3,4096]{0,1,2:T(4,128)(2,1)} %copy.17234), calls=%async_computation | async-start | bytes 8388608 | tf_op jit(solution)/shard_map/all_to_all | solution.py:110
  21.6 343.7 %all-reduce.4.cloned.1.call-start = ((), (), s32[]{:S(2)}) async-start(), calls=%async_computation.1 | async-start | bytes 2031616 | tf_op jit(solution)/shard_map/psum | solution.py:123
  205.0 9.4 %copy-start.2 = (f32[33,31,1536]{2,1,0:T(8,128)S(1)}, f32[33,31,1536]{2,1,0:T(8,128)}, u32[]{:S(2)}) copy-start(f32[33,31,1536]{2,1,0:T(8,128)} %squeeze.62) | copy-start | bytes 18855940
  205.0 9.4 %copy-start.3 = (f32[33,31,1536]{2,1,0:T(8,128)S(1)}, f32[33,31,1536]{2,1,0:T(8,128)}, u32[]{:S(2)}) copy-start(f32[33,31,1536]{2,1,0:T(8,128)} %squeeze.63) | copy-start | bytes 18855940
  368.8 54.7 %copy-start.4 = (f32[1,31,33]{2,0,1:T(1,128)}, f32[1,31,33]{2,0,1:T(1,128)S(1)}, u32[]{:S(2)}) copy-start(f32[1,31,33]{2,0,1:T(1,128)S(1)} %broadcast_select_fusion.55) | copy-start | bytes 12280
  448.5 8.1 %slice-start.2 = ((f32[1,31,33]{2,0,1:T(1,128)}), f32[1,28,33]{2,0,1:T(1,128)S(1)}, s32[]{:S(2)}) async-start(f32[1,31,33]{2,0,1:T(1,128)} %copy-done.4), calls=%async_computation.4 | async-start | bytes 28672 | tf_op jit(solution)/shard_map/slice | solution.py:83
  462.8 9.6 %copy-start.5 = (f32[31,31,33]{0,1,2:T(8,128)}, f32[31,31,33]{0,1,2:T(8,128)S(1)}, u32[]{:S(2)}) copy-start(f32[31,31,33]{0,1,2:T(8,128)S(1)} %copy.17831) | copy-start | bytes 380560
  473.2 10.2 %slice-start = ((s8[6488064]{0:T(1024)(128)(4,1)}), s8[2293760]{0:T(1024)(128)(4,1)S(1)}, s32[]{:S(2)}) async-start(s8[6488064]{0:T(1024)(128)(4,1)} %bitcast.633), calls=%async_computation.2 | async-start | bytes 4587520
  473.8 9.6 %slice-start.1 = ((s8[6488064]{0:T(1024)(128)(4,1)}), s8[4194304]{0:T(1024)(128)(4,1)S(1)}, s32[]{:S(2)}) async-start(s8[6488064]{0:T(1024)(128)(4,1)} %bitcast.633), calls=%async_computation.3 | async-start | bytes 8388608
  516.4 15.3 %copy-start.1 = (f32[16]{0:T(128)S(1)}, f32[16]{0:T(128)}, u32[]{:S(2)}) copy-start(f32[16]{0:T(128)} %param.7) | copy-start | bytes 196
Sparse Core Ops, SparseCore 0:
  236.7 128.5 all-reduce.3
where the time goes:
time: 546 us; the launch traced here: 539 us
  waiting for transfers between devices  221 us (40%)
  local copies, waits for them, and re-layouts  178 us (33%)
  matrix products  77.2 us (14%)
  other arithmetic  36 us (7%)
  between operations  19.3 us (4%)
  starting transfers between devices  7.32 us (1%)
    psum x1, waiting for transfers between devices, on_device(): sum_real, sum_imag = lax.psum((part_real, part_imag), ('pts', 'snap'))  129 us
    all_to_all x1, waiting for transfers between devices, on_device(): lax.all_to_all(snapshots, 'snap', split_axis=2, concat_axis=0, tiled=True)  92.2 us
    slice x3, local copies, waits for them, and re-layouts, gram(): amp_real, amp_imag = (amplitude[0], amplitude[1])  33.9 us
    unnamed x350, local copies, waits for them, and re-layouts  26 us
    squeeze x2, local copies, waits for them, and re-layouts, gram(): amp_real, amp_imag = (amplitude[0], amplitude[1])  23.2 us
    another operation x2, local copies, waits for them, and re-layouts, project(): return jnp.stack([mode_real, mode_imag])  14.5 us
    another operation x27, local copies, waits for them, and re-layouts, complex_cholesky(): done_real = jnp.stack(rows_real)  11.6 us
    gather x1, local copies, waits for them, and re-layouts, spectra(): lax.dynamic_slice_in_dim(series, offset, WIN, 0)  11.6 us
  transfers between devices with their start and end apart: 2, of which 2 were waited for; matrix products, arithmetic and copies ran while one was open for 0% of the time, Pallas kernels for 0%

commit v1 on v0

v1 whole, which is shorter than its diff:
```python
import functools
import math

import jax
import jax.numpy as jnp
from jax import lax
from jax.experimental import pallas as pl
from jax.experimental.pallas import tpu as pltpu
from jax.sharding import PartitionSpec as P

WIN = 64
NF = WIN // 2 + 1
ROWS = 32
HALF = ROWS // 2
GROUP = 11
PGROUP = 3
VMEM_LIMIT = 56 * 1024 * 1024


def make_table(length, freq_count):
    steps_time = jnp.arange(length, dtype=jnp.int32)
    freq_index = jnp.arange(freq_count, dtype=jnp.int32)
    phase_index = freq_index[:, None] * steps_time[None, :] % length
    angle_value = 2.0 * math.pi / length * phase_index.astype(jnp.float32)
    window = 0.5 - 0.5 * jnp.cos(2.0 * math.pi / length * steps_time.astype(jnp.float32))
    dft_table = jnp.stack(
        [window[None, :] * jnp.cos(angle_value), -window[None, :] * jnp.sin(angle_value)]
    ).astype(jnp.bfloat16)
    return dft_table


def spectrum_kernel(nt, index_ref, table_ref, root_ref, series_ref, amp_ref, gram_ref, band, sums_ref):
    comps = series_ref.shape[1]
    points = series_ref.shape[3]
    for chunk in range(nt // 128):
        lanes = slice(chunk * 128, (chunk + 1) * 128)
        where = index_ref[:, lanes]
        for j in range(GROUP):
            for k in range(2):
                source = jnp.broadcast_to(table_ref[j, k : k + 1, :], (ROWS, 128))
                values = jnp.take_along_axis(source, where, axis=1, mode="promise_in_bounds")
                row = (2 * j + k) * ROWS
                band[row : row + ROWS, lanes] = values.astype(jnp.bfloat16)
    for j in range(GROUP):
        for k in range(2):
            total = jnp.sum(table_ref[j, k : k + 1, :], axis=1, keepdims=True)
            row = (2 * j + k) * ROWS
            sums_ref[row : row + ROWS, :] = jnp.broadcast_to(total, (ROWS, 128))
    sums = sums_ref[:, 0:1]
    root = root_ref[...]
    ones = jnp.ones((16, nt), jnp.bfloat16)
    for c in range(comps):
        series = series_ref[:, c].reshape(nt, points)
        mean = jnp.dot(ones, series, preferred_element_type=jnp.float32)[0:1] / nt
        raw = jnp.dot(band[...], series, preferred_element_type=jnp.float32)
        amp = (raw - sums * mean) * root
        high = amp.astype(jnp.bfloat16)
        low = (amp - high.astype(jnp.float32)).astype(jnp.bfloat16)
        lanes = slice(c * points, (c + 1) * points)
        amp_ref[:, : 2 * ROWS, lanes] = high.reshape(GROUP, 2 * ROWS, points)
        amp_ref[:, 2 * ROWS :, lanes] = low.reshape(GROUP, 2 * ROWS, points)
    n = 2 * ROWS
    for j in range(GROUP):
        both = amp_ref[j]
        quad = lax.dot_general(both, both, (((1,), (1,)), ((), ())), preferred_element_type=jnp.float32)
        g = quad[:n, :n] + (quad[:n, n:] + quad[n:, :n]) + quad[n:, n:]
        real = g[:ROWS, :ROWS] + g[ROWS:, ROWS:]
        imag = g[:ROWS, ROWS:] - g[ROWS:, :ROWS]
        line = jnp.concatenate([real[:HALF], imag[:HALF], real[HALF:], imag[HALF:]], axis=1)
        gram_ref[:, pl.ds(pl.program_id(0) * GROUP + j, 1), :] = line.reshape(HALF, 1, 4 * ROWS)


def spectrum_call(series, index, table, root):
    parts, comps, times, points = series.shape
    nt = parts * times
    width = comps * points
    n = 2 * ROWS
    return pl.pallas_call(
        functools.partial(spectrum_kernel, nt),
        grid=(NF // GROUP,),
        in_specs=[
            pl.BlockSpec((ROWS, nt), lambda i: (0, 0)),
            pl.BlockSpec((GROUP, 2, 128), lambda i: (i, 0, 0)),
            pl.BlockSpec((1, points), lambda i: (0, 0)),
            pl.BlockSpec(series.shape, lambda i: (0, 0, 0, 0)),
        ],
        out_specs=[
            pl.BlockSpec((GROUP, 2 * n, width), lambda i: (i, 0, 0)),
            pl.BlockSpec((HALF, NF, 4 * ROWS), lambda i: (0, 0, 0)),
        ],
        out_shape=[
            jax.ShapeDtypeStruct((NF, 2 * n, width), jnp.bfloat16),
            jax.ShapeDtypeStruct((HALF, NF, 4 * ROWS), jnp.float32),
        ],
        scratch_shapes=[pltpu.VMEM((GROUP * n, nt), jnp.bfloat16), pltpu.VMEM((GROUP * n, 128), jnp.float32)],
        compiler_params=pltpu.CompilerParams(vmem_limit_bytes=VMEM_LIMIT),
        name="spectrum_gram",
    )(index, table, root, series)


def factor_kernel(nb, scale, gram_ref, r_ref, weight_ref, gr, gi, xr, xi, wide):
    wide[...] = jnp.zeros_like(wide)
    for q in range(HALF):
        wide[:NF, :] = gram_ref[q] * scale
        block = jnp.transpose(wide[...]).reshape(2, 2, ROWS, 128)
        gr[q], gi[q] = block[0, 0], block[0, 1]
        gr[q + HALF], gi[q + HALF] = block[1, 0], block[1, 1]
    shape = (ROWS, ROWS, 128)
    same = lax.broadcasted_iota(jnp.int32, shape, 0) == lax.broadcasted_iota(jnp.int32, shape, 1)
    xr[...] = same.astype(jnp.float32)
    xi[...] = jnp.zeros(shape, jnp.float32)
    used = lax.broadcasted_iota(jnp.int32, (1, 128), 1) < NF
    for i in range(nb):
        low = i // 8 * 8
        top = low + 8
        inverse = 1.0 / jnp.sqrt(jnp.where(used, gr[i, i : i + 1, :], 1.0))
        rr = gr[i, low:, :] * inverse
        ri = gi[i, low:, :] * inverse
        yr = xr[i, :top, :] * inverse
        yi = xi[i, :top, :] * inverse
        if i + 1 < nb:
            lr = gr[i + 1 : nb, i : i + 1, :] * inverse
            li = gi[i + 1 : nb, i : i + 1, :] * inverse
            gr[i + 1 : nb, low:, :] -= lr * rr[None] - li * ri[None]
            gi[i + 1 : nb, low:, :] -= lr * ri[None] + li * rr[None]
            xr[i + 1 : nb, :top, :] -= lr * yr[None] - li * yi[None]
            xi[i + 1 : nb, :top, :] -= lr * yi[None] + li * yr[None]
        column = lax.broadcasted_iota(jnp.int32, rr.shape, 0) + low
        if low:
            gr[i, :low, :] = jnp.zeros((low, 128), jnp.float32)
            gi[i, :low, :] = jnp.zeros((low, 128), jnp.float32)
        gr[i, low:, :] = jnp.where(column >= i, rr, 0.0)
        gi[i, low:, :] = jnp.where(column > i, ri, 0.0)
        xr[i, :top, :] = yr
        xi[i, :top, :] = yi


    r_ref[0] = gr[...]
    r_ref[1] = gi[...]
    for m in range(ROWS):
        real, imag = xr[m], xi[m]
        for k, pair in enumerate(([real, imag], [-imag, real])):
            lines = jnp.transpose(jnp.concatenate(pair + pair, axis=0))
            weight_ref[:, 2 * m + k : 2 * m + k + 1, :] = lines[:NF].reshape(NF, 1, 128)


def factor_call(gram, nb, scale):
    cube = pltpu.VMEM((ROWS, ROWS, 128), jnp.float32)
    return pl.pallas_call(
        functools.partial(factor_kernel, nb, scale),
        out_shape=[
            jax.ShapeDtypeStruct((2, ROWS, ROWS, 128), jnp.float32),
            jax.ShapeDtypeStruct((NF, 2 * ROWS, 4 * ROWS), jnp.float32),
        ],
        scratch_shapes=[cube, cube, cube, cube, pltpu.VMEM((128, 128), jnp.float32)],
        compiler_params=pltpu.CompilerParams(vmem_limit_bytes=VMEM_LIMIT),
        name="factor",
    )(gram)


def project_kernel(weight_ref, amp_ref, out_ref):
    n = 2 * ROWS
    points = out_ref.shape[4]
    for j in range(PGROUP):
        weight = weight_ref[j]
        high = weight.astype(jnp.bfloat16)
        low = (weight - high.astype(jnp.float32)).astype(jnp.bfloat16)
        modes = jnp.dot(high, amp_ref[j], preferred_element_type=jnp.float32)
        modes += jnp.dot(low[:, :n], amp_ref[j, :n, :], preferred_element_type=jnp.float32)
        modes = modes.astype(jnp.bfloat16)
        for c in range(out_ref.shape[2]):
            for m in range(out_ref.shape[1]):
                out_ref[j, m, c] = modes[2 * m : 2 * m + 2, c * points : (c + 1) * points]


def project_call(weight, amp, nb, comps):
    n = 2 * ROWS
    width = amp.shape[2]
    points = width // comps
    return pl.pallas_call(
        project_kernel,
        grid=(NF // PGROUP,),
        in_specs=[
            pl.BlockSpec((PGROUP, n, 2 * n), lambda i: (i, 0, 0)),
            pl.BlockSpec((PGROUP, 2 * n, width), lambda i: (i, 0, 0)),
        ],
        out_specs=pl.BlockSpec((PGROUP, nb, comps, 2, points), lambda i: (i, 0, 0, 0, 0)),
        out_shape=jax.ShapeDtypeStruct((NF, nb, comps, 2, points), jnp.bfloat16),
        compiler_params=pltpu.CompilerParams(vmem_limit_bytes=VMEM_LIMIT),
        name="project",
    )(weight, amp)


def allreduce_kernel(part_ref, out_ref, got1, got2, got3, send1, recv1, send2, recv2, send3, recv3):
    snap = lax.axis_size("snap")
    pts = lax.axis_size("pts")
    ms = lax.axis_index("snap")
    mp = lax.axis_index("pts")
    depth = part_ref.shape[0] // snap
    mesh_id = pl.DeviceIdType.MESH
    barrier = pltpu.get_barrier_semaphore()
    for d in range(1, snap):
        pl.semaphore_signal(barrier, inc=1, device_id=(mp, lax.rem(ms + d, snap)), device_id_type=mesh_id)
    for d in range(1, pts):
        pl.semaphore_signal(barrier, inc=1, device_id=(lax.rem(mp + d, pts), ms), device_id_type=mesh_id)
    pl.semaphore_wait(barrier, snap + pts - 2)

    copies = []
    for d in range(1, snap):
        to = lax.rem(ms + d, snap)
        copies.append(pltpu.make_async_remote_copy(
            src_ref=part_ref.at[pl.ds(to * depth, depth)], dst_ref=got1.at[d], send_sem=send1.at[d], recv_sem=recv1.at[d],
            device_id=(mp, to), device_id_type=mesh_id))
        copies[-1].start()
    total = part_ref[pl.ds(ms * depth, depth)]
    for d in range(1, snap):
        copies[d - 1].wait_recv()
        total = total + got1[d]
    got2[mp] = total
    cross = []
    for d in range(1, pts):
        cross.append(pltpu.make_async_remote_copy(
            src_ref=got2.at[mp], dst_ref=got2.at[mp], send_sem=send2.at[d], recv_sem=recv2.at[d],
            device_id=(lax.rem(mp + d, pts), ms), device_id_type=mesh_id))
        cross[-1].start()
    for copy in cross:
        copy.wait_recv()
    total = got2[0]
    for p in range(1, pts):
        total = total + got2[p]
    got3[ms] = total
    last = []
    for d in range(1, snap):
        last.append(pltpu.make_async_remote_copy(
            src_ref=got3.at[ms], dst_ref=got3.at[ms], send_sem=send3.at[d], recv_sem=recv3.at[d],
            device_id=(mp, lax.rem(ms + d, snap)), device_id_type=mesh_id))
        last[-1].start()
    for copy in last:
        copy.wait_recv()
    for p in range(snap):
        out_ref[p * depth : (p + 1) * depth] = got3[p]
    for copy in copies + cross + last:
        copy.wait_send()


def allreduce_call(part):
    snap = lax.axis_size("snap")
    pts = lax.axis_size("pts")
    slot = (part.shape[0] // snap,) + part.shape[1:]
    dma = pltpu.SemaphoreType.DMA
    return pl.pallas_call(
        allreduce_kernel,
        in_specs=[pl.BlockSpec(memory_space=pltpu.VMEM)],
        out_specs=pl.BlockSpec(memory_space=pltpu.VMEM),
        out_shape=jax.ShapeDtypeStruct(part.shape, part.dtype),
        scratch_shapes=[
            pltpu.VMEM((snap,) + slot, part.dtype),
            pltpu.VMEM((pts,) + slot, part.dtype),
            pltpu.VMEM((snap,) + slot, part.dtype),
            dma((snap,)), dma((snap,)), dma((pts,)), dma((pts,)), dma((snap,)), dma((snap,)),
        ],
        compiler_params=pltpu.CompilerParams(
            collective_id=0, has_side_effects=True, vmem_limit_bytes=VMEM_LIMIT),
        name="gram_sum",
    )(part)


def on_device(snapshots, block_starts, point_slab, slab_weight):
    size = lax.axis_size("snap")
    times, comps, wide_points = snapshots.shape
    points = wide_points // size
    nt = times * size
    nb = block_starts.shape[0]
    all_points = wide_points * lax.axis_size("pts")
    by_owner = jnp.transpose(snapshots.reshape(times, comps, size, points), (2, 1, 0, 3))
    series = lax.all_to_all(by_owner, "snap", split_axis=0, concat_axis=0, tiled=True)

    dft_table = make_table(WIN, NF)
    table = jnp.pad(jnp.moveaxis(dft_table, 0, 1).astype(jnp.float32), ((0, 0), (0, 0), (0, 128 - WIN)))
    starts = jnp.pad(block_starts, (0, ROWS - nb), constant_values=nt)
    offset = jnp.arange(nt, dtype=jnp.int32)[None, :] - starts[:, None]
    index = jnp.where((offset >= 0) & (offset < WIN), offset, WIN)
    slab_ids = jnp.arange(slab_weight.shape[0], dtype=jnp.int32)
    weights = jnp.sum(jnp.where(point_slab[:, None] == slab_ids[None, :], slab_weight[None, :], 0.0), axis=1)
    root = jnp.sqrt(weights / (0.375 * WIN))[None, :]

    amp, part = spectrum_call(series, index, table, root)
    gram = allreduce_call(part)
    r_cube, weight = factor_call(gram, nb, 1.0 / (3.0 * all_points))
    r_factor = jnp.transpose(r_cube[:, :nb, :nb, :NF], (0, 3, 1, 2))
    modes = project_call(weight, amp, nb, comps)
    mode_field = jnp.transpose(modes, (3, 0, 1, 2, 4))
    return (mode_field, r_factor)


def solution(mesh):
    in_specs = (P("snap", None, "pts"), P(), P(("pts", "snap")), P())
    out_specs = (P(None, None, None, None, ("pts", "snap")), P())
    return jax.shard_map(
        on_device, mesh=mesh, in_specs=in_specs, out_specs=out_specs, check_vma=False
    )
```

time: 546 us -> 149 us (0.27); the launches traced: 539 us -> 148 us
  local copies, waits for them, and re-layouts: 178 us -> 10.9 us
  waiting for transfers between devices: 221 us -> 68 us
  matrix products: 77.2 us -> 0 us
  Pallas kernels: 0 us -> 58.5 us
  other arithmetic: 36 us -> 2.71 us
  between operations: 19.3 us -> 0.69 us
    psum x1 -> x0, waiting for transfers between devices: 129 us -> none  [on_device(): sum_real, sum_imag = lax.psum((part_real, part_imag), ('pts', 'snap'))]
    dot_general x10 -> x0, matrix products: 77.2 us -> none  [the longest x1 11.4 us: spectra(): jnp.einsum('kfw,bwcp->kfbcp', dft_table, blocks, preferred_element_type=j...]
    another operation x119 -> x0, local copies, waits for them, and re-layouts: 60.7 us -> none  [the longest x2 14.5 us: project(): return jnp.stack([mode_real, mode_imag])]
    pallas_call x0 -> x4, Pallas kernels: none -> 58.5 us  [the longest x1 20.5 us: allreduce_call(): pl.pallas_call(allreduce_kernel, in_specs=[pl.BlockSpec(memory_space=pltp...]
    slice x66 -> x0, local copies, waits for them, and re-layouts: 34.1 us -> none  [the longest x3 33.9 us: gram(): amp_real, amp_imag = (amplitude[0], amplitude[1])]
    squeeze x31 -> x0, local copies, waits for them, and re-layouts: 26 us -> none  [the longest x2 23.2 us: gram(): amp_real, amp_imag = (amplitude[0], amplitude[1])]
    all_to_all x1, waiting for transfers between devices: 92.2 us -> 68 us  [on_device(): lax.all_to_all(by_owner, 'snap', split_axis=0, concat_axis=0, tiled=True)]
    unnamed x350 -> x10, local copies, waits for them, and re-layouts: 26 us -> 6.87 us
  transfers between devices with their start and end apart: 2 -> 1, of which waited for: 2 -> 1; matrix products, arithmetic and copies ran while one was open for 0% -> 2% of each run, Pallas kernels for 0% -> 0%
where the time goes in v1:
time: 149 us; the launch traced here: 148 us
  waiting for transfers between devices  68 us (46%)
  Pallas kernels  58.5 us (39%)
  local copies, waits for them, and re-layouts  10.9 us (7%)
  starting transfers between devices  7.41 us (5%)
  other arithmetic  2.71 us (2%)
    all_to_all x1, waiting for transfers between devices, on_device(): lax.all_to_all(by_owner, 'snap', split_axis=0, concat_axis=0, tiled=True)  68 us
    pallas_call x1, Pallas kernels, allreduce_call(): pl.pallas_call(allreduce_kernel, in_specs=[pl.BlockSpec(memory_space=pltp...  20.5 us
    pallas_call x1, Pallas kernels, spectrum_call(): pl.pallas_call(functools.partial(spectrum_kernel, nt), grid=(NF // GROUP,...  17.7 us
    pallas_call x1, Pallas kernels, project_call(): pl.pallas_call(project_kernel, grid=(NF // PGROUP,), in_specs=[pl.BlockSp...  13.5 us
    all_to_all x1, starting transfers between devices, on_device(): lax.all_to_all(by_owner, 'snap', split_axis=0, concat_axis=0, tiled=True)  7.41 us
    unnamed x10, local copies, waits for them, and re-layouts  6.87 us
    pallas_call x1, Pallas kernels, factor_call(): pl.pallas_call(functools.partial(factor_kernel, nb, scale), out_shape=[ja...  6.78 us
  transfers between devices with their start and end apart: 1, of which 1 were waited for; matrix products, arithmetic and copies ran while one was open for 2% of the time, Pallas kernels for 0%

profile of v1, /device:TPU:0, one launch (start us, length us, event | category | flops | bytes accessed | tf_op | source)
XLA Modules:
  0.0 148.2 jit_solution(13493533964382955434)
XLA Ops:
  0.6 3.5 %copy.10 = bf16[128,3,4096]{0,2,1:T(8,128)(2,1)S(1)} copy(bf16[128,3,4096]{2,0,1:T(8,128)(2,1)} %param.4) | data formatting | bytes 6291456 | tf_op args[0]
  4.1 2.8 %copy.11 = bf16[128,3,8,512]{3,0,1,2:T(8,128)(2,1)} copy(bf16[128,3,8,512]{0,3,2,1:T(8,128)(2,1)S(1)} %bitcast.9) | data formatting | bytes 6291456 | tf_op jit(solution)/shard_map/reshape | solution.py:275
  6.9 0.0 copy-start.3
  6.9 0.0 copy-start.1
  6.9 0.0 copy-start.2
  6.9 7.4 %all-to-all-start = ((bf16[8,3,128,512]{3,2,1,0:T(8,128)(2,1)}), bf16[8,3,128,512]{3,2,1,0:T(8,128)(2,1)S(1)}, u32[]{:S(2)}, u32[]{:S(2)}) async-start(bf16[8,3,128,512]{3,2,1,0:T(8,128)(2,1)} %bitcast.8), calls=%async_computation | async-start | bytes 6291456 | tf_op jit(solution)/shard_map/all_to_all | solution.py:276
  14.3 0.0 copy-done.3
  14.4 0.5 multiply_convert_fusion
  15.0 0.1 maximum_bitcast_fusion
  15.0 0.6 pad_convert_fusion.table_ref
  15.7 0.0 copy-done.1
  15.7 0.0 copy-done.2
  15.7 0.1 select_reduce_fusion
  15.8 0.6 multiply_sqrt_fusion
  16.3 0.8 fusion.index_ref
  17.1 68.0 %all-to-all-done.series_ref = bf16[8,3,128,512]{3,2,1,0:T(8,128)(2,1)S(1)} async-done(((bf16[8,3,128,512]{3,2,1,0:T(8,128)(2,1)}), bf16[8,3,128,512]{3,2,1,0:T(8,128)(2,1)S(1)}, u32[]{:S(2)}, u32[]{:S(2)}) %all-to-all-start) | async-done | bytes 3145760 | tf_op jit(solution)/shard_map/all_to_all | solution.py:276
  85.0 0.0 copy-start
  85.0 1.7 %copy-done = bf16[8,3,128,512]{3,2,1,0:T(8,128)(2,1)} copy-done((bf16[8,3,128,512]{3,2,1,0:T(8,128)(2,1)}, bf16[8,3,128,512]{3,2,1,0:T(8,128)(2,1)S(1)}, u32[]{:S(2)}) %copy-start) | copy-done | bytes 3145752
  86.7 17.7 %spectrum_gram.1 = (bf16[33,128,1536]{2,1,0:T(8,128)(2,1)}, f32[16,33,128]{2,1,0:T(8,128)}) custom-call(s32[32,1024]{1,0:T(8,128)} %fusion.index_ref, f32[33,2,128]{2,1,0:T(2,128)} %pad_convert_fusion.table_ref, f32[1,512]{1,0:T(1,128)} %bitcast.11, bf16[8,3,128,512]{3,2,1,0:T(8,128)(2,1)} %copy-done), custom_call_target="tpu_custom_call" | custom-call | tf_op jit(solution)/shard_map/spectrum_gram/pallas_call | solution.py:78
  104.4 20.5 %gram_sum.1.gram_ref = f32[16,33,128]{2,1,0:T(8,128)} custom-call(f32[16,33,128]{2,1,0:T(8,128)} %get-tuple-element.6.part_ref), custom_call_target="tpu_custom_call" | custom-call | tf_op jit(solution)/shard_map/gram_sum/pallas_call | solution.py:251
  124.9 6.8 %factor.1 = (f32[2,32,32,128]{3,2,1,0:T(8,128)}, f32[33,64,128]{2,1,0:T(8,128)}) custom-call(f32[16,33,128]{2,1,0:T(8,128)} %gram_sum.1.gram_ref), custom_call_target="tpu_custom_call" | custom-call | tf_op jit(solution)/shard_map/factor/pallas_call | solution.py:149
  131.7 1.3 slice_bitcast_fusion
  133.0 1.7 %copy.12 = f32[2,33,31,31]{1,0,3,2:T(2,128)} copy(f32[2,33,31,31]{1,3,2,0:T(8,128)S(1)} %slice_bitcast_fusion) | data formatting | bytes 507408
  134.7 13.5 %project.1 = bf16[33,31,3,2,512]{4,3,2,1,0:T(2,128)(2,1)} custom-call(f32[33,64,128]{2,1,0:T(8,128)} %get-tuple-element.7.weight_ref, bf16[33,128,1536]{2,1,0:T(8,128)(2,1)} %get-tuple-element.8.amp_ref), custom_call_target="tpu_custom_call" | custom-call | tf_op jit(solution)/shard_map/project/pallas_call | solution.py:180
  (3 shorter events, 0.1 us)
Async XLA Ops:
  6.9 7.4 %copy-start.3 = (s32[31]{0:T(128)S(1)}, s32[31]{0:T(128)}, u32[]{:S(2)}) copy-start(s32[31]{0:T(128)} %param.5) | copy-start | bytes 376
  6.9 8.8 %copy-start.1 = (s32[512]{0:T(512)S(1)}, s32[512]{0:T(512)}, u32[]{:S(2)}) copy-start(s32[512]{0:T(512)} %param.6) | copy-start | bytes 6148
  6.9 8.8 %copy-start.2 = (f32[16]{0:T(128)S(1)}, f32[16]{0:T(128)}, u32[]{:S(2)}) copy-start(f32[16]{0:T(128)} %param.7) | copy-start | bytes 196
  6.9 78.1 %all-to-all-start = ((bf16[8,3,128,512]{3,2,1,0:T(8,128)(2,1)}), bf16[8,3,128,512]{3,2,1,0:T(8,128)(2,1)S(1)}, u32[]{:S(2)}, u32[]{:S(2)}) async-start(bf16[8,3,128,512]{3,2,1,0:T(8,128)(2,1)} %bitcast.8), calls=%async_computation | async-start | bytes 6291456 | tf_op jit(solution)/shard_map/all_to_all | solution.py:276
  85.0 1.7 %copy-start = (bf16[8,3,128,512]{3,2,1,0:T(8,128)(2,1)}, bf16[8,3,128,512]{3,2,1,0:T(8,128)(2,1)S(1)}, u32[]{:S(2)}) copy-start(bf16[8,3,128,512]{3,2,1,0:T(8,128)(2,1)S(1)} %all-to-all-done.series_ref) | copy-start | bytes 9437188

commit v2 on v1

--- a/solution.py
+++ b/solution.py
@@ -29,73 +29,138 @@
     return dft_table
 
 
-def spectrum_kernel(nt, index_ref, table_ref, root_ref, series_ref, amp_ref, gram_ref, band, sums_ref):
-    comps = series_ref.shape[1]
-    points = series_ref.shape[3]
-    for chunk in range(nt // 128):
-        lanes = slice(chunk * 128, (chunk + 1) * 128)
-        where = index_ref[:, lanes]
-        for j in range(GROUP):
-            for k in range(2):
-                source = jnp.broadcast_to(table_ref[j, k : k + 1, :], (ROWS, 128))
-                values = jnp.take_along_axis(source, where, axis=1, mode="promise_in_bounds")
-                row = (2 * j + k) * ROWS
-                band[row : row + ROWS, lanes] = values.astype(jnp.bfloat16)
+def band_kernel(nt, index_ref, table_ref, band_ref, sums_ref):
     for j in range(GROUP):
         for k in range(2):
-            total = jnp.sum(table_ref[j, k : k + 1, :], axis=1, keepdims=True)
+            line = table_ref[j, k : k + 1, :]
+            source = jnp.broadcast_to(line, (ROWS, 128))
             row = (2 * j + k) * ROWS
+            for chunk in range(nt // 128):
+                lanes = slice(chunk * 128, (chunk + 1) * 128)
+                values = jnp.take_along_axis(source, index_ref[:, lanes], axis=1, mode="promise_in_bounds")
+                band_ref[row : row + ROWS, lanes] = values.astype(jnp.bfloat16)
+            total = jnp.sum(line, axis=1, keepdims=True)
             sums_ref[row : row + ROWS, :] = jnp.broadcast_to(total, (ROWS, 128))
-    sums = sums_ref[:, 0:1]
-    root = root_ref[...]
-    ones = jnp.ones((16, nt), jnp.bfloat16)
-    for c in range(comps):
-        series = series_ref[:, c].reshape(nt, points)
-        mean = jnp.dot(ones, series, preferred_element_type=jnp.float32)[0:1] / nt
-        raw = jnp.dot(band[...], series, preferred_element_type=jnp.float32)
-        amp = (raw - sums * mean) * root
-        high = amp.astype(jnp.bfloat16)
-        low = (amp - high.astype(jnp.float32)).astype(jnp.bfloat16)
-        lanes = slice(c * points, (c + 1) * points)
-        amp_ref[:, : 2 * ROWS, lanes] = high.reshape(GROUP, 2 * ROWS, points)
-        amp_ref[:, 2 * ROWS :, lanes] = low.reshape(GROUP, 2 * ROWS, points)
-    n = 2 * ROWS
-    for j in range(GROUP):
-        both = amp_ref[j]
-        quad = lax.dot_general(both, both, (((1,), (1,)), ((), ())), preferred_element_type=jnp.float32)
-        g = quad[:n, :n] + (quad[:n, n:] + quad[n:, :n]) + quad[n:, n:]
-        real = g[:ROWS, :ROWS] + g[ROWS:, ROWS:]
-        imag = g[:ROWS, ROWS:] - g[ROWS:, :ROWS]
-        line = jnp.concatenate([real[:HALF], imag[:HALF], real[HALF:], imag[HALF:]], axis=1)
-        gram_ref[:, pl.ds(pl.program_id(0) * GROUP + j, 1), :] = line.reshape(HALF, 1, 4 * ROWS)
-
-
-def spectrum_call(series, index, table, root):
-    parts, comps, times, points = series.shape
-    nt = parts * times
-    width = comps * points
-    n = 2 * ROWS
-    return pl.pallas_call(
-        functools.partial(spectrum_kernel, nt),
+
+
+def band_call(index, table):
+    nt = index.shape[1]
+    rows = GROUP * 2 * ROWS
+    return pl.pallas_call(
+        functools.partial(band_kernel, nt),
         grid=(NF // GROUP,),
         in_specs=[
             pl.BlockSpec((ROWS, nt), lambda i: (0, 0)),
             pl.BlockSpec((GROUP, 2, 128), lambda i: (i, 0, 0)),
-            pl.BlockSpec((1, points), lambda i: (0, 0)),
-            pl.BlockSpec(series.shape, lambda i: (0, 0, 0, 0)),
         ],
         out_specs=[
-            pl.BlockSpec((GROUP, 2 * n, width), lambda i: (i, 0, 0)),
-            pl.BlockSpec((HALF, NF, 4 * ROWS), lambda i: (0, 0, 0)),
-        ],
+            pl.BlockSpec((rows, nt), lambda i: (i, 0)),
+            pl.BlockSpec((rows, 128), lambda i: (i, 0)),
+        ],
+        out_shape=[
+            jax.ShapeDtypeStruct((NF * 2 * ROWS, nt), jnp.bfloat16),
+            jax.ShapeDtypeStruct((NF * 2 * ROWS, 128), jnp.float32),
+        ],
+        compiler_params=pltpu.CompilerParams(vmem_limit_bytes=VMEM_LIMIT),
+        name="band",
+    )(index, table)
+
+
+def spectrum_kernel(
+    band_ref, sums_ref, root_ref, snap_ref, amp_ref, gram_ref, series, amp, send, recv, own, store
+):
+    snap = lax.axis_size("snap")
+    ms = lax.axis_index("snap")
+    mp = lax.axis_index("pts")
+    mesh_id = pl.DeviceIdType.MESH
+    comps, _, times, points = series.shape
+    nt = snap * times
+    n = 2 * ROWS
+    barrier = pltpu.get_barrier_semaphore()
+    for d in range(1, snap):
+        pl.semaphore_signal(barrier, inc=1, device_id=(mp, lax.rem(ms + d, snap)), device_id_type=mesh_id)
+    pl.semaphore_wait(barrier, snap - 1)
+
+    kept, sent, stored = [], [], []
+    for c in range(comps):
+        mine = pl.ds(pl.multiple_of(ms * points, points), points)
+        kept.append(pltpu.make_async_copy(snap_ref.at[c, :, mine], series.at[c, ms], own.at[c]))
+        kept[c].start()
+        sent.append([])
+        for d in range(1, snap):
+            to = lax.rem(ms + d, snap)
+            theirs = pl.ds(pl.multiple_of(to * points, points), points)
+            copy = pltpu.make_async_remote_copy(
+                src_ref=snap_ref.at[c, :, theirs], dst_ref=series.at[c, ms],
+                send_sem=send.at[c, d], recv_sem=recv.at[c, d],
+                device_id=(mp, to), device_id_type=mesh_id)
+            copy.start()
+            sent[c].append(copy)
+
+    gram_ref[...] = jnp.zeros_like(gram_ref)
+    root = root_ref[...]
+    ones = jnp.ones((16, nt), jnp.bfloat16)
+    for c in range(comps):
+        kept[c].wait()
+        for copy in sent[c]:
+            copy.wait_recv()
+        lanes = slice(c * points, (c + 1) * points)
+        mean = jnp.dot(ones, series[c].reshape(nt, points), preferred_element_type=jnp.float32)[0:1] / nt
+
+        def group_step(g, _):
+            rows = pl.ds(pl.multiple_of(g * (GROUP * n), GROUP * n), GROUP * n)
+            raw = jnp.dot(band_ref[rows, :], series[c].reshape(nt, points), preferred_element_type=jnp.float32)
+            value = (raw - sums_ref[rows, 0:1] * mean) * root
+            high = value.astype(jnp.bfloat16)
+            low = (value - high.astype(jnp.float32)).astype(jnp.bfloat16)
+            amp[pl.ds(g * GROUP, GROUP), :n, lanes] = high.reshape(GROUP, n, points)
+            amp[pl.ds(g * GROUP, GROUP), n:, lanes] = low.reshape(GROUP, n, points)
+            for j in range(GROUP):
+                f = g * GROUP + j
+                both = amp[f, :, lanes]
+                quad = lax.dot_general(both, both, (((1,), (1,)), ((), ())), preferred_element_type=jnp.float32)
+                full = quad[:n, :n] + (quad[:n, n:] + quad[n:, :n]) + quad[n:, n:]
+                real = full[:ROWS, :ROWS] + full[ROWS:, ROWS:]
+                imag = full[:ROWS, ROWS:] - full[ROWS:, :ROWS]
+                line = jnp.concatenate([real[:HALF], imag[:HALF], real[HALF:], imag[HALF:]], axis=1)
+                gram_ref[:, pl.ds(f, 1), :] += line.reshape(HALF, 1, 4 * ROWS)
+            return 0
+
+        lax.fori_loop(0, NF // GROUP, group_step, 0)
+        stored.append(pltpu.make_async_copy(amp.at[:, :, lanes], amp_ref.at[:, :, lanes], store.at[c]))
+        stored[c].start()
+    for c in range(comps):
+        stored[c].wait()
+        for copy in sent[c]:
+            copy.wait_send()
+
+
+def spectrum_call(snapshots, band, sums, root):
+    comps, times, wide_points = snapshots.shape
+    snap = lax.axis_size("snap")
+    points = wide_points // snap
+    width = comps * points
+    n = 2 * ROWS
+    dma = pltpu.SemaphoreType.DMA
+    vmem = pl.BlockSpec(memory_space=pltpu.VMEM)
+    hbm = pl.BlockSpec(memory_space=pl.ANY)
+    return pl.pallas_call(
+        spectrum_kernel,
+        in_specs=[vmem, vmem, vmem, hbm],
+        out_specs=[hbm, vmem],
         out_shape=[
             jax.ShapeDtypeStruct((NF, 2 * n, width), jnp.bfloat16),
             jax.ShapeDtypeStruct((HALF, NF, 4 * ROWS), jnp.float32),
         ],
-        scratch_shapes=[pltpu.VMEM((GROUP * n, nt), jnp.bfloat16), pltpu.VMEM((GROUP * n, 128), jnp.float32)],
-        compiler_params=pltpu.CompilerParams(vmem_limit_bytes=VMEM_LIMIT),
+        scratch_shapes=[
+            pltpu.VMEM((comps, snap, times, points), jnp.bfloat16),
+            pltpu.VMEM((NF, 2 * n, width), jnp.bfloat16),
+            dma((comps, snap)), dma((comps, snap)), dma((comps,)), dma((comps,)),
+        ],
+        compiler_params=pltpu.CompilerParams(
+            collective_id=1, has_side_effects=True, vmem_limit_bytes=VMEM_LIMIT),
         name="spectrum_gram",
-    )(index, table, root, series)
+    )(band, sums, root, snapshots)
 
 
 def factor_kernel(nb, scale, gram_ref, r_ref, weight_ref, gr, gi, xr, xi, wide):
@@ -272,9 +337,6 @@
     nt = times * size
     nb = block_starts.shape[0]
     all_points = wide_points * lax.axis_size("pts")
-    by_owner = jnp.transpose(snapshots.reshape(times, comps, size, points), (2, 1, 0, 3))
-    series = lax.all_to_all(by_owner, "snap", split_axis=0, concat_axis=0, tiled=True)
-
     dft_table = make_table(WIN, NF)
     table = jnp.pad(jnp.moveaxis(dft_table, 0, 1).astype(jnp.float32), ((0, 0), (0, 0), (0, 128 - WIN)))
     starts = jnp.pad(block_starts, (0, ROWS - nb), constant_values=nt)
@@ -284,7 +346,8 @@
     weights = jnp.sum(jnp.where(point_slab[:, None] == slab_ids[None, :], slab_weight[None, :], 0.0), axis=1)
     root = jnp.sqrt(weights / (0.375 * WIN))[None, :]
 
-    amp, part = spectrum_call(series, index, table, root)
+    band, sums = band_call(index, table)
+    amp, part = spectrum_call(jnp.transpose(snapshots, (1, 0, 2)), band, sums, root)
     gram = allreduce_call(part)
     r_cube, weight = factor_call(gram, nb, 1.0 / (3.0 * all_points))
     r_factor = jnp.transpose(r_cube[:, :nb, :nb, :NF], (0, 3, 1, 2))

time: 149 us -> 143 us (0.960)
  Pallas kernels: 58.5 us -> 136 us
  waiting for transfers between devices: 68 us -> 0 us
  local copies, waits for them, and re-layouts: 10.9 us -> 2.44 us
  starting transfers between devices: 7.41 us -> 0 us
    pallas_call x1 -> x2, Pallas kernels: 17.7 us -> 86.6 us  [the longest x1 76.9 us: spectrum_call(): pl.pallas_call(spectrum_kernel, in_specs=[vmem, vmem, vmem, hbm], out_spe...]
    all_to_all x1 -> x0, waiting for transfers between devices: 68 us -> none  [on_device(): lax.all_to_all(by_owner, 'snap', split_axis=0, concat_axis=0, tiled=True)]
    pallas_call x1, Pallas kernels: 20.5 us -> 28.9 us  [allreduce_call(): pl.pallas_call(allreduce_kernel, in_specs=[pl.BlockSpec(memory_space=pltp...]
    all_to_all x1 -> x0, starting transfers between devices: 7.41 us -> none  [on_device(): lax.all_to_all(by_owner, 'snap', split_axis=0, concat_axis=0, tiled=True)]
    unnamed x10 -> x3, local copies, waits for them, and re-layouts: 6.87 us -> 1.72 us
    reshape x1 -> x0, local copies, waits for them, and re-layouts: 2.77 us -> none  [on_device(): snapshots.reshape(times, comps, size, points)]
  transfers between devices with their start and end apart: 1 -> 0, of which waited for: 1 -> 0; matrix products, arithmetic and copies ran while one was open for 2% -> 0% of each run, Pallas kernels for 0% -> 0%
where the time goes in v2:
time: 143 us; the launch traced here: 142 us
  Pallas kernels  136 us (95%)
  other arithmetic  3.45 us (2%)
  local copies, waits for them, and re-layouts  2.44 us (2%)
    pallas_call x1, Pallas kernels, spectrum_call(): pl.pallas_call(spectrum_kernel, in_specs=[vmem, vmem, vmem, hbm], out_spe...  76.9 us
    pallas_call x1, Pallas kernels, allreduce_call(): pl.pallas_call(allreduce_kernel, in_specs=[pl.BlockSpec(memory_space=pltp...  28.9 us
    pallas_call x1, Pallas kernels, project_call(): pl.pallas_call(project_kernel, grid=(NF // PGROUP,), in_specs=[pl.BlockSp...  13.6 us
    pallas_call x1, Pallas kernels, band_call(): pl.pallas_call(functools.partial(band_kernel, nt), grid=(NF // GROUP,), i...  9.65 us
    pallas_call x1, Pallas kernels, factor_call(): pl.pallas_call(functools.partial(factor_kernel, nb, scale), out_shape=[ja...  6.76 us

profile of v2, /device:TPU:0, one launch (start us, length us, event | category | flops | bytes accessed | tf_op | source)
XLA Modules:
  0.0 142.4 jit_solution(7015189263302471211)
XLA Ops:
  0.6 0.7 pad.10
  1.4 0.8 select_reduce_fusion
  2.2 0.6 multiply_sqrt_fusion
  2.8 0.5 multiply_convert_fusion
  3.3 0.1 maximum_bitcast_fusion
  3.4 0.6 pad_convert_fusion.table_ref
  4.0 0.7 fusion.index_ref
  4.8 9.6 %band.1 = (bf16[2112,1024]{1,0:T(8,128)(2,1)}, f32[2112,128]{1,0:T(8,128)}) custom-call(s32[32,1024]{1,0:T(8,128)} %fusion.index_ref, f32[33,2,128]{2,1,0:T(2,128)} %pad_convert_fusion.table_ref), custom_call_target="tpu_custom_call" | custom-call | tf_op jit(solution)/shard_map/band/pallas_call | solution.py:49
  14.4 76.9 %spectrum_gram.1 = (bf16[33,128,1536]{2,1,0:T(8,128)(2,1)}, f32[16,33,128]{2,1,0:T(8,128)}) custom-call(bf16[2112,1024]{1,0:T(8,128)(2,1)} %get-tuple-element.8.band_ref, f32[2112,128]{1,0:T(8,128)} %get-tuple-element.9.sums_ref, f32[1,512]{1,0:T(1,128)} %bitcast.9, bf16[3,128,4096]{2,1,0:T(8,128)(2,1)} %bitcast.8), custom_call_target="tpu_custom_call" | custom-call | tf_op jit(solution)/shard_map/spectrum_gram/pallas_call | solution.py:147
  91.3 28.9 %gram_sum.1.gram_ref = f32[16,33,128]{2,1,0:T(8,128)} custom-call(f32[16,33,128]{2,1,0:T(8,128)} %get-tuple-element.10.part_ref), custom_call_target="tpu_custom_call" | custom-call | tf_op jit(solution)/shard_map/gram_sum/pallas_call | solution.py:316
  120.3 6.8 %factor.1 = (f32[2,32,32,128]{3,2,1,0:T(8,128)}, f32[33,64,128]{2,1,0:T(8,128)}) custom-call(f32[16,33,128]{2,1,0:T(8,128)} %gram_sum.1.gram_ref), custom_call_target="tpu_custom_call" | custom-call | tf_op jit(solution)/shard_map/factor/pallas_call | solution.py:214
  127.0 0.0 copy-start
  127.0 13.6 %project.1 = bf16[33,31,3,2,512]{4,3,2,1,0:T(2,128)(2,1)} custom-call(f32[33,64,128]{2,1,0:T(8,128)} %get-tuple-element.11.weight_ref, bf16[33,128,1536]{2,1,0:T(8,128)(2,1)} %get-tuple-element.12.amp_ref), custom_call_target="tpu_custom_call" | custom-call | tf_op jit(solution)/shard_map/project/pallas_call | solution.py:245
  140.7 0.0 copy-done
  140.7 0.1 slice_bitcast_fusion
  140.7 1.7 %copy.7 = f32[2,33,31,31]{1,0,3,2:T(2,128)} copy(f32[2,33,31,31]{1,3,2,0:T(8,128)S(1)} %slice_bitcast_fusion) | data formatting | bytes 507408
  (2 shorter events, 0.1 us)
Async XLA Ops:
  127.0 13.6 %copy-start = (f32[2,32,32,128]{3,2,1,0:T(8,128)S(1)}, f32[2,32,32,128]{3,2,1,0:T(8,128)}, u32[]{:S(2)}) copy-start(f32[2,32,32,128]{3,2,1,0:T(8,128)} %get-tuple-element.13) | copy-start | bytes 3145732
